TPU v7x, 512 devices: a whole 4x8x8 slice. The times are simulated.
512 devices in a mesh: ax: 64 (over x, y_hi, z), circ: 8 (over y_lo, core).
Axes of the slice: x: 4, y: 8 (y_hi: 2, y_lo: 4; y = y_hi * 4 + y_lo), z: 8, core: 2. Of those that a mesh axis runs over, the one named last changes fastest.
Arguments:
- lam_start: bfloat16 [64, 42, 3072], P('ax', None, 'circ'), may hold values from -6 to 6
- rhs: bfloat16 [64, 42, 3072], P('ax', None, 'circ'), may hold values from -6 to 6
- state: bfloat16 [64, 42, 3072], P('ax', None, 'circ'), may hold values from -6 to 6
- blocks: bfloat16 [64, 96, 768], P('ax'), may hold values from -0.21875 to 0.21875
- slots: int32 [64, 8], P('ax'), may hold values from 0 to 8, as said below
- mass: float32 [64, 96], P('ax'), may hold values from 0.5 to 2
- precond: float32 [64, 96], P('ax'), may hold values from 0.2 to 0.6
- contact_blocks: bfloat16 [32768, 9216], P(('ax', 'circ')), may hold values from -0.625 to 0.625
- contact_flags: int32 [32768, 128], P(('ax', 'circ')), may hold values 0 or 1
- contact_owner: int32 [32768], P(('ax', 'circ')), may hold values from 0 to 63, as said below
- contact_row: int32 [32768], P(('ax', 'circ')), may hold values from 0 to 3
- contact_front: int32 [32768], P(('ax', 'circ')), may hold values from 0 to 1023
Outputs:
- adjoint: float32 [64, 42, 3072], P('ax', None, 'circ')
- sensitivity: float32 [1024], P('ax')
Inputs may be any that keep to these rules, and one draw needn't show every extreme that they name: `slots`: each row lists 8 distinct codes, one of them 4; code c names the block at axial offset c // 3 - 1 and circumferential offset c mod 3 - 1. `contact_owner`: of the 64 contacts held by one device, at most 2 name any one section; for the devices that share a circ index, one section is named by exactly 2 contacts of every one of them.
All inputs are finite; a program needn't handle non-finite values. No bound on the sum of `contact_flags` on one device may be relied on, other than what follows from the above.
Results may differ from a plain program's by a relative error of at most 0.0032.
Values may be sent and summed in bfloat16 or wider, within the bound.
A program may use at most 64 MiB of HBM per device.

v0:
```python
import math

import jax
import jax.numpy as jnp
from jax import lax
from jax.sharding import PartitionSpec as P

SAMPLES = 128
FPD = 16


omega_rate = 0.05
sens_scale = 0.015625


def with_halo(block, sides, width, periodic):
    for axis, dim in sides:
        count = lax.axis_size(axis)
        forward = [(i, i + 1) for i in range(count - 1)]
        if periodic:
            forward.append((count - 1, 0))
        backward = [(target, source) for source, target in forward]
        low = lax.ppermute(
            lax.slice_in_dim(block, block.shape[dim] - width, None, axis=dim), axis, forward
        )
        high = lax.ppermute(lax.slice_in_dim(block, 0, width, axis=dim), axis, backward)
        block = jnp.concatenate([low, block, high], axis=dim)
    return block


def time_table(samples, columns):
    moments = jnp.arange(samples).astype(jnp.float32)[:, None]
    column_ids = jnp.arange(columns, dtype=jnp.int32)[None, :]
    orders = (column_ids // 2 + 1).astype(jnp.float32)
    phases = 2.0 * math.pi / samples * moments * orders
    return jnp.where(column_ids % 2 == 0, jnp.cos(phases), jnp.sin(phases))


def harmonic_filters(flag_rows, time_rows):
    weighted = flag_rows.astype(jnp.float32)[:, :, None] * time_rows[None, :, :]
    return (
        2.0
        / time_rows.shape[0]
        * jnp.einsum("kth,tg->khg", weighted, time_rows, precision=lax.Precision.HIGHEST)
    )


def mass_factors(columns):
    orders = (jnp.arange(columns, dtype=jnp.int32) // 2 + 1).astype(jnp.float32)
    return (omega_rate * orders) ** 2


def pick_rows(field_rows, wanted, sector_cols):
    shaped = field_rows.reshape(field_rows.shape[0], field_rows.shape[1], sector_cols, -1)
    chosen = shaped[wanted // sector_cols, :, wanted % sector_cols, :]
    return jnp.transpose(chosen, (1, 0, 2))


def add_rows(accumulated, wanted, values, sector_cols):
    shaped = accumulated.reshape(accumulated.shape[0], accumulated.shape[1], sector_cols, -1)
    shaped = shaped.at[wanted // sector_cols, :, wanted % sector_cols, :].add(
        jnp.transpose(values, (1, 0, 2))
    )
    return shaped.reshape(accumulated.shape)


def adjoint_effect(picked, blocks_flat, filters):
    block_width = picked.shape[2]
    square = blocks_flat.reshape(blocks_flat.shape[0], block_width, block_width)
    coupled = jnp.einsum("gkq,kqp->gkp", picked, square, preferred_element_type=jnp.float32)
    return jnp.einsum("khg,gkp->hkp", filters, coupled, precision=lax.Precision.HIGHEST)


def forward_effect(picked, blocks_flat, filters):
    block_width = picked.shape[2]
    square = blocks_flat.reshape(blocks_flat.shape[0], block_width, block_width)
    coupled = jnp.einsum("gkq,kpq->gkp", picked, square, preferred_element_type=jnp.float32)
    return jnp.einsum("khg,gkp->hkp", filters, coupled, precision=lax.Precision.HIGHEST)


def place_slots(owners, capacity, owner_count):
    onehot = (owners[:, None] == jnp.arange(owner_count, dtype=jnp.int32)[None, :]).astype(
        jnp.int32
    )
    before = jnp.cumsum(onehot, axis=0) - onehot
    slot_rank = jnp.sum(before * onehot, axis=1)
    return owners * capacity + slot_rank


def stiffness_terms(extended, blocks, slots, sector_cols):
    block_width = blocks.shape[1]
    harmonics = extended.shape[1]
    zero_index = jnp.zeros((), jnp.int32)
    pieces = []
    for slot_index in range(slots.shape[1]):
        slot_code = slots[0, slot_index]
        start_row = slot_code // 3 + 0
        start_col = slot_code % 3 * block_width
        block_slice = lax.dynamic_slice(
            extended, (start_row, zero_index, start_col), (1, harmonics, sector_cols * block_width)
        )
        pieces.append(block_slice.reshape(harmonics, sector_cols, block_width))
    gathered = [jnp.stack(pieces, axis=2).reshape(harmonics * sector_cols, -1)]
    stacked = jnp.stack(gathered, axis=0)
    product = jnp.einsum("amk,apk->amp", stacked, blocks, preferred_element_type=jnp.float32)
    return product.reshape(blocks.shape[0], harmonics, sector_cols * block_width)


def shards(
    lam_start,
    rhs,
    state,
    blocks,
    slots,
    mass,
    precond,
    contact_blocks,
    contact_flags,
    contact_owner,
    contact_row,
    contact_front,
):
    harmonics = lam_start.shape[1]
    block_width = blocks.shape[1]
    sector_cols = lam_start.shape[2] // block_width
    sections = lax.axis_size("ax")
    capacity = max(2, 2 * contact_owner.shape[0] // sections)
    slots_total = sections * capacity
    time_rows = time_table(SAMPLES, harmonics)
    factors = mass_factors(harmonics)
    mass_term = factors[None, :, None] * jnp.tile(mass, (1, sector_cols))[:, None, :]
    relaxation = jnp.tile(precond, (1, sector_cols))[:, None, :]
    rhs_full = rhs.astype(jnp.float32)
    destination = place_slots(contact_owner, capacity, sections)
    block_buffer = (
        jnp.zeros((slots_total, contact_blocks.shape[1]), jnp.bfloat16)
        .at[destination]
        .set(contact_blocks)
    )
    flag_buffer = (
        jnp.zeros((slots_total, contact_flags.shape[1]), jnp.int32)
        .at[destination]
        .set(contact_flags)
    )
    row_buffer = jnp.zeros((slots_total,), jnp.int32).at[destination].set(contact_row)
    front_buffer = jnp.zeros((slots_total,), jnp.int32).at[destination].set(contact_front)
    held_blocks, held_flags, held_rows, held_fronts = (
        lax.all_to_all(block_buffer, "ax", split_axis=0, concat_axis=0, tiled=True),
        lax.all_to_all(flag_buffer, "ax", split_axis=0, concat_axis=0, tiled=True),
        lax.all_to_all(row_buffer, "ax", split_axis=0, concat_axis=0, tiled=True),
        lax.all_to_all(front_buffer, "ax", split_axis=0, concat_axis=0, tiled=True),
    )
    held_filters = harmonic_filters(held_flags, time_rows)

    def contact_sum(lowered):
        picked = pick_rows(lowered, held_rows, sector_cols)
        effect = adjoint_effect(picked, held_blocks, held_filters)
        return add_rows(jnp.zeros(lowered.shape, jnp.float32), held_rows, effect, sector_cols)

    def relax_sweep(current, lowered):
        sector_padded = with_halo(lowered, (("circ", 2),), block_width, True)
        extended = with_halo(sector_padded, (("ax", 0),), 1, False)
        applied = (
            stiffness_terms(extended, blocks, slots, sector_cols)
            - mass_term * current
            + contact_sum(lowered)
        )
        return current + relaxation * (rhs_full - applied)

    halfway = relax_sweep(lam_start.astype(jnp.float32), lam_start)
    adjoint = relax_sweep(halfway, halfway.astype(jnp.bfloat16))
    picked_state = pick_rows(state, held_rows, sector_cols)
    picked_adjoint = pick_rows(adjoint.astype(jnp.bfloat16), held_rows, sector_cols)
    effect = forward_effect(picked_state, held_blocks, held_filters)
    front_parts = -sens_scale * jnp.sum(picked_adjoint.astype(jnp.float32) * effect, axis=(0, 2))
    front_parts, fronts = (front_parts, held_fronts)
    partial_sums = jnp.zeros((FPD * sections,), jnp.float32).at[fronts].add(front_parts)
    totals = lax.psum(partial_sums, ("ax", "circ"))
    sensitivity = lax.dynamic_slice_in_dim(totals, lax.axis_index("ax") * FPD, FPD)
    return (adjoint, sensitivity)


def solution(mesh):
    in_specs = (
        P("ax", None, "circ"),
        P("ax", None, "circ"),
        P("ax", None, "circ"),
        P("ax", None, None),
        P("ax", None),
        P("ax", None),
        P("ax", None),
        P(("ax", "circ"), None),
        P(("ax", "circ"), None),
        P(("ax", "circ")),
        P(("ax", "circ")),
        P(("ax", "circ")),
    )
    out_specs = (P("ax", None, "circ"), P("ax"))
    return jax.shard_map(shards, mesh=mesh, in_specs=in_specs, out_specs=out_specs, check_vma=False)
```

profile of v0, /device:TPU:1, one launch (start us, length us, event | category | flops | bytes accessed | tf_op | source)
XLA Modules:
  0.0 379.8 jit_solution(5400270008125155318)
XLA Ops:
  4.7 19.6 %all-to-all-start = ((s32[64,2,1]{1,2,0:T(1,128)}), s32[64,2,1]{1,2,0:T(1,128)S(1)}, u32[]{:S(2)}, u32[]{:S(2)}) async-start(s32[64,2,1]{1,2,0:T(1,128)} %bitcast.27), calls=%async_computation | async-start | bytes 65536 | tf_op jit(solution)/shard_map/all_to_all | solution.py:150
  25.9 11.4 %all-to-all-done = s32[64,2,1]{1,2,0:T(1,128)S(1)} async-done(((s32[64,2,1]{1,2,0:T(1,128)}), s32[64,2,1]{1,2,0:T(1,128)S(1)}, u32[]{:S(2)}, u32[]{:S(2)}) %all-to-all-start) | async-done | bytes 544 | tf_op jit(solution)/shard_map/all_to_all | solution.py:150
  37.4 4.6 %all-to-all-start.3 = ((s32[64,2,1]{1,2,0:T(1,128)}), s32[64,2,1]{1,2,0:T(1,128)S(1)}, u32[]{:S(2)}, u32[]{:S(2)}) async-start(s32[64,2,1]{1,2,0:T(1,128)} %bitcast.37), calls=%async_computation.3 | async-start | bytes 65536 | tf_op jit(solution)/shard_map/all_to_all | solution.py:151
  43.5 11.6 %all-to-all-done.3 = s32[64,2,1]{1,2,0:T(1,128)S(1)} async-done(((s32[64,2,1]{1,2,0:T(1,128)}), s32[64,2,1]{1,2,0:T(1,128)S(1)}, u32[]{:S(2)}, u32[]{:S(2)}) %all-to-all-start.3) | async-done | bytes 544 | tf_op jit(solution)/shard_map/all_to_all | solution.py:151
  55.1 4.6 %all-to-all-start.1 = ((s32[64,2,128]{2,1,0:T(2,128)}), s32[64,2,128]{2,1,0:T(2,128)S(1)}, u32[]{:S(2)}, u32[]{:S(2)}) async-start(s32[64,2,128]{2,1,0:T(2,128)} %bitcast.29), calls=%async_computation.1 | async-start | bytes 131072 | tf_op jit(solution)/shard_map/all_to_all | solution.py:149
  59.7 3.7 scatter_custom_fusion.2
  65.8 7.1 %all-to-all-done.1 = s32[64,2,128]{2,1,0:T(2,128)S(1)} async-done(((s32[64,2,128]{2,1,0:T(2,128)}), s32[64,2,128]{2,1,0:T(2,128)S(1)}, u32[]{:S(2)}, u32[]{:S(2)}) %all-to-all-start.1) | async-done | bytes 65568 | tf_op jit(solution)/shard_map/all_to_all | solution.py:149
  72.9 7.9 %all-to-all-start.2 = ((bf16[64,2,9216]{2,1,0:T(2,128)(2,1)}), bf16[64,2,9216]{2,1,0:T(2,128)(2,1)}, u32[]{:S(2)}, u32[]{:S(2)}) async-start(bf16[64,2,9216]{2,1,0:T(2,128)(2,1)} %all_to_all.33), calls=%async_computation.2 | async-start | bytes 4718592 | tf_op jit(solution)/shard_map/all_to_all | solution.py:148
  80.9 6.0 %collective-permute-start = (bf16[1,42,96]{2,1,0:T(8,128)(2,1)S(1)}, bf16[1,42,96]{2,1,0:T(8,128)(2,1)S(1)}, u32[]{:S(2)}, u32[]{:S(2)}) collective-permute-start(bf16[1,42,96]{2,1,0:T(8,128)(2,1)S(1)} %get-tuple-element.31), channel_id=1, source_target_pairs={{0,1},{1,2},{2,3},{3,4},{4,5},{5,6},{6,7},{7,0},{8,9},{9,10},{10,1... | collective-permute-start | bytes 24200 | tf_op jit(solution)/shard_map/ppermute | solution.py:23
  107.9 8.0 %collective-permute-done = bf16[1,42,96]{2,1,0:T(8,128)(2,1)S(1)} collective-permute-done((bf16[1,42,96]{2,1,0:T(8,128)(2,1)S(1)}, bf16[1,42,96]{2,1,0:T(8,128)(2,1)S(1)}, u32[]{:S(2)}, u32[]{:S(2)}) %collective-permute-start) | collective-permute-done | bytes 8096 | tf_op jit(solution)/shard_map/ppermute | solution.py:23
  115.9 18.3 %collective-permute-done.1 = bf16[1,42,96]{2,1,0:T(8,128)(2,1)S(1)} collective-permute-done((bf16[1,42,96]{2,1,0:T(8,128)(2,1)S(1)}, bf16[1,42,96]{2,1,0:T(8,128)(2,1)S(1)}, u32[]{:S(2)}, u32[]{:S(2)}) %collective-permute-start.1) | collective-permute-done | bytes 8096 | tf_op jit(solution)/shard_map/ppermute | solution.py:26
  134.3 3.6 collective-permute-start.2
  145.9 4.1 %fusion.17 = f32[128,42,42]{0,2,1:T(8,128)} fusion(f32[128,42]{0,1:T(8,128)S(1)} %fusion.38, f32[128,128]{1,0:T(8,128)S(1)} %bitcast.84), kind=kOutput, calls=%fused_computation.29 | convolution fusion | flops 347730432 | bytes 990208 | tf_op jit(solution)/shard_map/kth,tg->khg/dot_general | solution.py:44
  152.2 7.0 %reshape.462 = bf16[128,96,96]{2,1,0:T(8,128)(2,1)} reshape(bf16[64,2,9216]{2,1,0:T(2,128)(2,1)} %all-to-all-done.2) | data formatting | bytes 4718592 | tf_op jit(solution)/shard_map/reshape | solution.py:69
  159.3 3.3 fusion.13
  162.5 5.1 %fusion.5 = f32[128,42,96]{2,1,0:T(8,128)} fusion(f32[128,42,42]{2,1,0:T(8,128)S(1)} %copy.42, f32[128,96,42]{1,2,0:T(8,128)S(1)} %fusion.13), kind=kOutput, calls=%fused_computation.17 | convolution fusion | flops 260112384 | bytes 5031936 | tf_op jit(solution)/shard_map/khg,gkp->hkp/dot_general | solution.py:71
  167.6 12.8 %scatter_fusion = f32[42,4,96]{2,0,1:T(8,128)S(1)} fusion(f32[42,4,96]{2,0,1:T(8,128)S(1)} %broadcast.404.clone, s32[128]{0:T(128)S(1)} %get-tuple-element.41, f32[128,42,96]{2,1,0:T(8,128)} %fusion.5), kind=kCustom, calls=%fused_computation.7 | custom fusion | flops 516096 | bytes 6193664 | tf_op jit(solution)/shard_map/scatter-add | solution.py:61
  191.8 3.3 fusion.11
  195.1 5.1 %fusion.3 = f32[128,42,96]{2,1,0:T(8,128)} fusion(f32[128,42,42]{2,1,0:T(8,128)S(1)} %copy.42, f32[128,96,42]{1,2,0:T(8,128)S(1)} %fusion.11), kind=kOutput, calls=%fused_computation.15 | convolution fusion | flops 260112384 | bytes 5031936 | tf_op jit(solution)/shard_map/khg,gkp->hkp/dot_general | solution.py:71
  200.9 4.8 %collective-permute-start.6 = (bf16[1,42,576]{2,1,0:T(8,128)(2,1)}, bf16[1,42,576]{2,1,0:T(8,128)(2,1)}, u32[]{:S(2)}, u32[]{:S(2)}) collective-permute-start(bf16[1,42,576]{2,1,0:T(8,128)(2,1)} %pad_maximum_fusion.3), channel_id=1, source_target_pairs={{0,8},{8,16},{16,24},{24,32},{32,40},{40,48},{48,56},{56,64},{64,7... | collective-permute-start | bytes 145160 | tf_op jit(solution)/shard_map/ppermute | solution.py:23
  207.0 3.8 %fusion.9 = f32[128,96,42]{1,2,0:T(8,128)} fusion(bf16[128,96,96]{2,1,0:T(8,128)(2,1)S(1)} %copy-done.1, bf16[128,42,96]{2,1,0:T(8,128)(2,1)S(1)} %copy-done.2), kind=kOutput, calls=%fused_computation.21 | convolution fusion | flops 99090432 | bytes 5455872 | tf_op jit(solution)/shard_map/gkq,kpq->gkp/dot_general | solution.py:77
  210.9 13.0 %scatter_fusion.1 = f32[42,4,96]{2,0,1:T(8,128)S(1)} fusion(f32[42,4,96]{2,0,1:T(8,128)S(1)} %broadcast.404, s32[128]{0:T(128)} %copy-done.14, f32[128,42,96]{2,1,0:T(8,128)} %fusion.3), kind=kCustom, calls=%fused_computation.8 | custom fusion | flops 516096 | bytes 6193664 | tf_op jit(solution)/shard_map/scatter-add | solution.py:61
  261.4 5.9 %fusion = f32[128]{0:T(128)S(1)} fusion(bf16[128,42,96]{2,1,0:T(8,128)(2,1)} %gather_fusion.2, f32[128,42,42]{2,1,0:T(8,128)S(1)} %copy.42, f32[128,96,42]{1,2,0:T(8,128)} %fusion.9), kind=kOutput, calls=%fused_computation.12 | convolution fusion | flops 261660544 | bytes 4000256 | tf_op jit(solution)/shard_map/khg,gkp->hkp/dot_general | solution.py:78
  268.9 109.7 %psum.7 = f32[1024]{0:T(1024)S(1)} all-reduce(f32[1024]{0:T(1024)S(1)} %scatter_custom_fusion.6), channel_id=1, replica_groups=mesh['ax'=64,'circ'=8] {'ax','circ'}, use_global_device_ids=true, to_apply=%region_10.11 | all-reduce | flops 1024 | bytes 8192 | tf_op jit(solution)/shard_map/psum | solution.py:178
  (151 shorter events, 78.8 us)
Async XLA Ops:
  0.6 144.9 %copy-start = (bf16[1,96,768]{2,1,0:T(8,128)(2,1)S(1)}, bf16[1,96,768]{2,1,0:T(8,128)(2,1)}, u32[]{:S(2)}) copy-start(bf16[1,96,768]{2,1,0:T(8,128)(2,1)} %param.15) | copy-start | bytes 442372
  4.7 32.7 %all-to-all-start = ((s32[64,2,1]{1,2,0:T(1,128)}), s32[64,2,1]{1,2,0:T(1,128)S(1)}, u32[]{:S(2)}, u32[]{:S(2)}) async-start(s32[64,2,1]{1,2,0:T(1,128)} %bitcast.27), calls=%async_computation | async-start | bytes 65536 | tf_op jit(solution)/shard_map/all_to_all | solution.py:150
  37.4 17.8 %all-to-all-start.3 = ((s32[64,2,1]{1,2,0:T(1,128)}), s32[64,2,1]{1,2,0:T(1,128)S(1)}, u32[]{:S(2)}, u32[]{:S(2)}) async-start(s32[64,2,1]{1,2,0:T(1,128)} %bitcast.37), calls=%async_computation.3 | async-start | bytes 65536 | tf_op jit(solution)/shard_map/all_to_all | solution.py:151
  55.1 17.8 %all-to-all-start.1 = ((s32[64,2,128]{2,1,0:T(2,128)}), s32[64,2,128]{2,1,0:T(2,128)S(1)}, u32[]{:S(2)}, u32[]{:S(2)}) async-start(s32[64,2,128]{2,1,0:T(2,128)} %bitcast.29), calls=%async_computation.1 | async-start | bytes 131072 | tf_op jit(solution)/shard_map/all_to_all | solution.py:149
  65.8 39.2 %copy-start.17 = (f32[1,96]{1,0:T(1,128)S(1)}, f32[1,96]{1,0:T(1,128)}, u32[]{:S(2)}) copy-start(f32[1,96]{1,0:T(1,128)} %param.17) | copy-start | bytes 1156
  65.8 39.3 %copy-start.18 = (f32[1,96]{1,0:T(1,128)S(1)}, f32[1,96]{1,0:T(1,128)}, u32[]{:S(2)}) copy-start(f32[1,96]{1,0:T(1,128)} %param.18) | copy-start | bytes 1156
  65.8 39.4 %copy-start.8 = (bf16[1,42,384]{2,1,0:T(8,128)(2,1)S(1)}, bf16[1,42,384]{2,1,0:T(8,128)(2,1)}, u32[]{:S(2)}) copy-start(bf16[1,42,384]{2,1,0:T(8,128)(2,1)} %param.14) | copy-start | bytes 96772
  72.9 79.3 %all-to-all-start.2 = ((bf16[64,2,9216]{2,1,0:T(2,128)(2,1)}), bf16[64,2,9216]{2,1,0:T(2,128)(2,1)}, u32[]{:S(2)}, u32[]{:S(2)}) async-start(bf16[64,2,9216]{2,1,0:T(2,128)(2,1)} %all_to_all.33), calls=%async_computation.2 | async-start | bytes 4718592 | tf_op jit(solution)/shard_map/all_to_all | solution.py:148
  80.9 35.0 %collective-permute-start = (bf16[1,42,96]{2,1,0:T(8,128)(2,1)S(1)}, bf16[1,42,96]{2,1,0:T(8,128)(2,1)S(1)}, u32[]{:S(2)}, u32[]{:S(2)}) collective-permute-start(bf16[1,42,96]{2,1,0:T(8,128)(2,1)S(1)} %get-tuple-element.31), channel_id=1, source_target_pairs={{0,1},{1,2},{2,3},{3,4},{4,5},{5,6},{6,7},{7,0},{8,9},{9,10},{10,1... | collective-permute-start | bytes 24200 | tf_op jit(solution)/shard_map/ppermute | solution.py:23
  86.8 47.4 %collective-permute-start.1 = (bf16[1,42,96]{2,1,0:T(8,128)(2,1)S(1)}, bf16[1,42,96]{2,1,0:T(8,128)(2,1)S(1)}, u32[]{:S(2)}, u32[]{:S(2)}) collective-permute-start(bf16[1,42,96]{2,1,0:T(8,128)(2,1)S(1)} %get-tuple-element.32), channel_id=1, source_target_pairs={{1,0},{2,1},{3,2},{4,3},{5,4},{6,5},{7,6},{0,7},{9,8},{10,9},{11,1... | collective-permute-start | bytes 24200 | tf_op jit(solution)/shard_map/ppermute | solution.py:26
  105.1 77.1 %copy-start.10 = (f32[384]{0:T(512)}, f32[384]{0:T(512)S(1)}, u32[]{:S(2)}) copy-start(f32[384]{0:T(512)S(1)} %mul.173) | copy-start | bytes 4612
  105.2 77.0 %copy-start.12 = (f32[384]{0:T(512)}, f32[384]{0:T(512)S(1)}, u32[]{:S(2)}) copy-start(f32[384]{0:T(512)S(1)} %tile.20) | copy-start | bytes 4612
  105.5 76.7 %copy-start.15 = (f32[42]{0:T(128)}, f32[42]{0:T(128)S(1)}, u32[]{:S(2)}) copy-start(f32[42]{0:T(128)S(1)} %multiply_multiply_fusion.2) | copy-start | bytes 508
  134.3 9.6 %collective-permute-start.2 = (bf16[1,42,576]{2,1,0:T(8,128)(2,1)S(1)}, bf16[1,42,576]{2,1,0:T(8,128)(2,1)S(1)}, u32[]{:S(2)}, u32[]{:S(2)}) collective-permute-start(bf16[1,42,576]{2,1,0:T(8,128)(2,1)S(1)} %pad_maximum_fusion.2), channel_id=1, source_target_pairs={{0,8},{8,16},{16,24},{24,32},{32,40},{40,48},{48,56},{56,64},{64,7... | collective-permute-start | bytes 145160 | tf_op jit(solution)/shard_map/ppermute | solution.py:23
  137.9 5.9 %collective-permute-start.3 = (bf16[1,42,576]{2,1,0:T(8,128)(2,1)S(1)}, bf16[1,42,576]{2,1,0:T(8,128)(2,1)S(1)}, u32[]{:S(2)}, u32[]{:S(2)}) collective-permute-start(bf16[1,42,576]{2,1,0:T(8,128)(2,1)S(1)} %pad_maximum_fusion.2), channel_id=1, source_target_pairs={{8,0},{16,8},{24,16},{32,24},{40,32},{48,40},{56,48},{64,56},{72,6... | collective-permute-start | bytes 145160 | tf_op jit(solution)/shard_map/ppermute | solution.py:26
  184.5 15.7 %collective-permute-start.4 = (bf16[1,42,96]{2,1,0:T(8,128)(2,1)}, bf16[1,42,96]{2,1,0:T(8,128)(2,1)S(1)}, u32[]{:S(2)}, u32[]{:S(2)}) collective-permute-start(bf16[1,42,96]{2,1,0:T(8,128)(2,1)} %get-tuple-element.29), channel_id=1, source_target_pairs={{0,1},{1,2},{2,3},{3,4},{4,5},{5,6},{6,7},{7,0},{8,9},{9,10},{10,1... | collective-permute-start | bytes 24200 | tf_op jit(solution)/shard_map/ppermute | solution.py:23
  186.4 13.8 %collective-permute-start.5 = (bf16[1,42,96]{2,1,0:T(8,128)(2,1)S(1)}, bf16[1,42,96]{2,1,0:T(8,128)(2,1)S(1)}, u32[]{:S(2)}, u32[]{:S(2)}) collective-permute-start(bf16[1,42,96]{2,1,0:T(8,128)(2,1)S(1)} %get-tuple-element.30), channel_id=1, source_target_pairs={{1,0},{2,1},{3,2},{4,3},{5,4},{6,5},{7,6},{0,7},{9,8},{10,9},{11,1... | collective-permute-start | bytes 24200 | tf_op jit(solution)/shard_map/ppermute | solution.py:26
  200.9 25.3 %collective-permute-start.6 = (bf16[1,42,576]{2,1,0:T(8,128)(2,1)}, bf16[1,42,576]{2,1,0:T(8,128)(2,1)}, u32[]{:S(2)}, u32[]{:S(2)}) collective-permute-start(bf16[1,42,576]{2,1,0:T(8,128)(2,1)} %pad_maximum_fusion.3), channel_id=1, source_target_pairs={{0,8},{8,16},{16,24},{24,32},{32,40},{40,48},{48,56},{56,64},{64,7... | collective-permute-start | bytes 145160 | tf_op jit(solution)/shard_map/ppermute | solution.py:23
  205.7 20.5 %collective-permute-start.7 = (bf16[1,42,576]{2,1,0:T(8,128)(2,1)}, bf16[1,42,576]{2,1,0:T(8,128)(2,1)}, u32[]{:S(2)}, u32[]{:S(2)}) collective-permute-start(bf16[1,42,576]{2,1,0:T(8,128)(2,1)} %pad_maximum_fusion.3), channel_id=1, source_target_pairs={{8,0},{16,8},{24,16},{32,24},{40,32},{48,40},{56,48},{64,56},{72,6... | collective-permute-start | bytes 145160 | tf_op jit(solution)/shard_map/ppermute | solution.py:26
  224.5 33.1 %copy-start.5 = (f32[1,42,384]{2,1,0:T(8,128)S(1)}, f32[1,42,384]{2,1,0:T(8,128)}, u32[]{:S(2)}) copy-start(f32[1,42,384]{2,1,0:T(8,128)} %copy-done.4) | copy-start | bytes 193540
  224.5 33.1 %copy-start.11 = (f32[384]{0:T(512)S(1)}, f32[384]{0:T(512)}, u32[]{:S(2)}) copy-start(f32[384]{0:T(512)} %copy-done.10) | copy-start | bytes 4612
  224.5 33.1 %copy-start.13 = (f32[384]{0:T(512)S(1)}, f32[384]{0:T(512)}, u32[]{:S(2)}) copy-start(f32[384]{0:T(512)} %copy-done.12) | copy-start | bytes 4612
  224.5 33.1 %copy-start.16 = (f32[42]{0:T(128)S(1)}, f32[42]{0:T(128)}, u32[]{:S(2)}) copy-start(f32[42]{0:T(128)} %copy-done.15) | copy-start | bytes 508
  261.4 117.2 %copy-start.6 = (f32[1,42,384]{2,1,0:T(8,128)S(1)}, f32[1,42,384]{2,1,0:T(8,128)}, u32[]{:S(2)}) copy-start(f32[1,42,384]{2,1,0:T(8,128)} %get-tuple-element.9) | copy-start | bytes 193540
  (7 other events, 100.7 us)
where the time goes:
time: 383 us; the launch traced here: 380 us
  blocking collectives  110 us (29%)
  local copies, waits for them, and re-layouts  67.7 us (18%)
  starting transfers between devices  60.3 us (16%)
  waiting for transfers between devices  56.4 us (15%)
  other arithmetic  36.4 us (10%)
  matrix products  32.6 us (9%)
  between operations  16.8 us (4%)
    psum x1, blocking collectives, shards(): totals = lax.psum(partial_sums, ('ax', 'circ'))  110 us
    scatter-add x2, other arithmetic, add_rows(): shaped.at[wanted // sector_cols, :, wanted % sector_cols, :]  25.8 us
    all_to_all x1, starting transfers between devices, shards(): lax.all_to_all(row_buffer, 'ax', split_axis=0, concat_axis=0, tiled=True)  19.6 us
    ppermute x4, waiting for transfers between devices, with_halo(): lax.ppermute(lax.slice_in_dim(block, 0, width, axis=dim), axis, backward)  18.3 us
    ppermute x4, starting transfers between devices, with_halo(): lax.ppermute(lax.slice_in_dim(block, block.shape[dim] - width, None, axis...  16.3 us
    another operation x20, local copies, waits for them, and re-layouts, stiffness_terms(): gathered = [jnp.stack(pieces, axis=2).reshape(harmonics * sector_cols, -1)]  15.1 us
    all_to_all x1, waiting for transfers between devices, shards(): lax.all_to_all(front_buffer, 'ax', split_axis=0, concat_axis=0, tiled=True)  11.6 us
    all_to_all x1, waiting for transfers between devices, shards(): lax.all_to_all(row_buffer, 'ax', split_axis=0, concat_axis=0, tiled=True)  11.4 us
  transfers between devices with their start and end apart: 12, of which 5 were waited for; matrix products, arithmetic and copies ran while one was open for 14% of the time, Pallas kernels for 0%

commit v1 on v0

v1 whole, which is shorter than its diff:
```python
import math

import jax
import jax.numpy as jnp
import numpy as np
from jax import lax
from jax.experimental import pallas as pl
from jax.experimental.pallas import tpu as pltpu
from jax.sharding import PartitionSpec as P

BLK = 96
HARM = 42
SAMPLES = 128
NNZ = 8
RC = 4
CPD = 64
SECTIONS = 64
SECTORS = 8
SLOTS = 2 * SECTIONS
STEP = 29
GROUP = 4

omega_rate = 0.05
sens_scale = 0.015625

F32 = jnp.float32
BF16 = jnp.bfloat16
HIGHEST = lax.Precision.HIGHEST
MESH = pl.DeviceIdType.MESH


def time_table():
    moments = np.arange(SAMPLES)[:, None]
    columns = np.arange(48)[None, :]
    phases = (2.0 * math.pi / SAMPLES) * ((moments * (columns // 2 + 1)) % SAMPLES)
    rows = np.where(columns % 2 == 0, np.cos(phases), np.sin(phases))
    rows[:, HARM:] = 0.0
    return rows.T.astype(np.float32)


def iota(shape, dim):
    return lax.broadcasted_iota(jnp.int32, shape, dim)


def dot(a, b, dims, precision=None):
    return lax.dot_general(a, b, (dims, ((), ())), precision=precision, preferred_element_type=F32)


NT = ((1,), (1,))
NN = ((1,), (0,))


def kernel(
    lam_ref, rhs_ref, state_ref, blocks_ref, slots_ref, mass_ref, precond_ref, contacts_ref,
    flags_ref, owner_ref, row_ref, front_ref, table_ref,
    adj_ref, sens_ref,
    idx_v, idx_s, meta_out, meta_in, send_buf, recv_buf, unpack, turned, chosen, acc, codes, fronts,
    onehot_lo, onehot_hi, rhs_buf, cur, base, ext1, ext2, wide, state_pad, xw, yw, bw, sums,
    part_a, recv_a, part_b, recv_b, part_c, recv_c,
    local_sem, meta_send, meta_recv, block_send, block_recv, halo_send, halo_recv,
    a_send, a_recv, b_send, b_recv, c_send, c_recv,
):
    ax = lax.axis_index("ax")
    ci = lax.axis_index("circ")
    xy, zz = ax // 8, lax.rem(ax, 8)

    def offset(i):
        return lax.rem(i * STEP, SECTIONS)

    def ax_peer(i):
        return lax.rem(ax + offset(i), SECTIONS)

    def around(da, dc):
        return (lax.rem(ax + da + SECTIONS, SECTIONS), lax.rem(ci + dc + SECTORS, SECTORS))

    corners = [(1, 1), (1, -1), (-1, 1), (-1, -1)]
    barrier = pltpu.get_barrier_semaphore()

    def greet(i, carry):
        pl.semaphore_signal(barrier, inc=1, device_id=(ax_peer(i), ci), device_id_type=MESH)
        return carry

    lax.fori_loop(1, SECTIONS, greet, 0)

    def greet_circ(j, carry):
        pl.semaphore_signal(barrier, inc=1, device_id=(ax, lax.rem(ci + j, SECTORS)), device_id_type=MESH)
        return carry

    lax.fori_loop(1, SECTORS, greet_circ, 0)
    for da, dc in corners:
        pl.semaphore_signal(barrier, inc=1, device_id=around(da, dc), device_id_type=MESH)

    eye64 = (iota((CPD, CPD), 0) == iota((CPD, CPD), 1)).astype(jnp.int32)

    def column(row):
        return jnp.sum(eye64 * row, axis=1, keepdims=True)

    owner_row = owner_ref[...]
    owner_col = column(owner_row)
    row_col = column(row_ref[...])
    front_col = column(front_ref[...])
    same = (owner_col == owner_row).astype(jnp.int32)
    below = (iota((CPD, CPD), 0) < iota((CPD, CPD), 1)).astype(jnp.int32)
    above = (iota((CPD, CPD), 1) < iota((CPD, CPD), 0)).astype(jnp.int32)
    dest_row = 2 * owner_row + jnp.sum(same * below, axis=0, keepdims=True)
    dest_col = 2 * owner_col + jnp.sum(same * above, axis=1, keepdims=True)
    hit = (dest_col == iota((CPD, SLOTS), 1)).astype(jnp.int32)
    index_row = jnp.sum(hit * iota((CPD, SLOTS), 0), axis=0, keepdims=True)
    idx_v[...] = jnp.broadcast_to(index_row, (8, SLOTS))
    to_scalar = pltpu.make_async_copy(idx_v, idx_s, local_sem.at[0])
    to_scalar.start()

    line = iota((8 * SECTIONS, CPD), 0)
    slot_of_line = 2 * (line // 8) + lax.rem(line, 2)
    kind_of_line = lax.rem(line, 8) // 2
    picks = dest_row == slot_of_line
    pick_codes = (picks & (kind_of_line == 0)).astype(BF16)
    pick_fronts = (picks & (kind_of_line == 1)).astype(BF16)
    coded = (flags_ref[...] * (row_col + 1)).astype(F32).astype(BF16)
    numbered = jnp.where(iota((CPD, 128), 1) < 64, front_col // 32, lax.rem(front_col, 32)).astype(F32).astype(BF16)
    meta = dot(pick_codes, coded, NN) + dot(pick_fronts, numbered, NN)
    meta_out[...] = meta.reshape(SECTIONS, 8, 128).astype(BF16)

    def pad_rows(ref, source):
        ref[...] = jnp.zeros(ref.shape, ref.dtype)
        for r in range(RC):
            ref[r, 0:HARM, 0:BLK] = source[0, :, r * BLK : (r + 1) * BLK].astype(F32)

    pad_rows(cur, lam_ref)
    ext1[1, 1:5] = cur[...].astype(BF16)

    pl.semaphore_wait(barrier, SECTIONS - 1 + SECTORS - 1 + len(corners))

    def halo(ext, sweep):
        moves = [
            (ext.at[1, 1:5], ext.at[0, 1:5], (1, 0)),
            (ext.at[1, 1:5], ext.at[2, 1:5], (-1, 0)),
            (ext.at[1, 4], ext.at[1, 0], (0, 1)),
            (ext.at[1, 1], ext.at[1, 5], (0, -1)),
            (ext.at[1, 4], ext.at[0, 0], (1, 1)),
            (ext.at[1, 1], ext.at[0, 5], (1, -1)),
            (ext.at[1, 4], ext.at[2, 0], (-1, 1)),
            (ext.at[1, 1], ext.at[2, 5], (-1, -1)),
        ]
        return [
            pltpu.make_async_remote_copy(
                src_ref=source, dst_ref=target, send_sem=halo_send.at[sweep, n], recv_sem=halo_recv.at[sweep, n],
                device_id=around(*way), device_id_type=MESH,
            )
            for n, (source, target, way) in enumerate(moves)
        ]

    halo1 = halo(ext1, 0)
    for copy in halo1:
        copy.start()

    def meta_copy(i):
        return pltpu.make_async_remote_copy(
            src_ref=meta_out.at[ax_peer(i)], dst_ref=meta_in.at[i], send_sem=meta_send.at[i],
            recv_sem=meta_recv.at[i], device_id=(ax_peer(i), ci), device_id_type=MESH,
        )

    def block_copy(i):
        return pltpu.make_async_remote_copy(
            src_ref=send_buf.at[i], dst_ref=recv_buf.at[i], send_sem=block_send.at[i],
            recv_sem=block_recv.at[i], device_id=(ax_peer(i), ci), device_id_type=MESH,
        )

    def start_meta(i, carry):
        meta_copy(i).start()
        return carry

    to_scalar.wait()

    def start_block(i, carry):
        slot = 2 * ax_peer(i)
        send_buf[i, 0:24, :] = contacts_ref[idx_s[0, slot]]
        send_buf[i, 24:48, :] = contacts_ref[idx_s[0, slot + 1]]
        block_copy(i).start()
        return carry

    lax.fori_loop(1, 9, start_block, 0)
    lax.fori_loop(1, SECTIONS, start_meta, 0)
    lax.fori_loop(9, SECTIONS, start_block, 0)
    recv_buf[0, 0:24, :] = contacts_ref[idx_s[0, 2 * ax]]
    recv_buf[0, 24:48, :] = contacts_ref[idx_s[0, 2 * ax + 1]]
    meta_in[0] = meta_out[ax]

    spot = iota((128, 128), 0)
    mixed = (iota((128, 128), 1) == 4 * lax.rem(spot, 24) + spot // 24) & (spot < BLK)
    mixer = mixed.astype(BF16)
    plain = (iota((128, 128), 1) == spot).astype(BF16)
    table = table_ref[...]
    table_hi = table.astype(BF16)
    table_lo = (table - table_hi.astype(F32)).astype(BF16)

    def spread(rows, order):
        turn = dot(order, rows, NT).astype(BF16)
        return dot(turn, table_hi, NN) + dot(turn, table_lo, NN)

    pad_rows(state_pad, state_ref)
    for r in range(RC):
        lanes = slice(r * SAMPLES, (r + 1) * SAMPLES)
        xw[:, lanes] = spread(ext1[1, 1 + r], mixer).astype(BF16)
        yw[:, lanes] = spread(state_pad[r].astype(BF16), plain).astype(BF16)
    pad_rows(rhs_buf, rhs_ref)
    wide[...] = jnp.zeros(wide.shape, F32)
    for s in range(NNZ):
        wide[s, :, 0:BLK] = blocks_ref[0, :, s * BLK : (s + 1) * BLK].astype(F32)
    acc[...] = jnp.zeros(acc.shape, F32)
    unpack[...] = jnp.zeros(unpack.shape, F32)

    def wait_meta(i, carry):
        meta_copy(i).wait_recv()
        return carry

    lax.fori_loop(1, SECTIONS, wait_meta, 0)

    def spread_meta(i, carry):
        rows = meta_in[i].astype(F32)
        codes[pl.ds(2 * i, 2), :] = rows[0:2]
        fronts[pl.ds(2 * i, 2), :] = rows[2:4]
        return carry

    lax.fori_loop(0, SECTIONS, spread_meta, 0)
    eye128 = (spot == iota((128, 128), 1)).astype(F32)
    high, low = fronts[:, 0:1], fronts[:, 64:65]
    major = jnp.floor(high * 0.25)
    minor = (high - 4.0 * major) * 32.0 + low
    onehot_lo[...] = (minor == iota((128, 128), 1).astype(F32)).astype(F32)
    major_row = jnp.sum(eye128 * major, axis=0, keepdims=True)
    onehot_hi[...] = (major_row == iota((8, 128), 0).astype(F32)).astype(F32)

    precond = precond_ref[...]
    harmonic = (iota((48, BLK), 0) // 2 + 1).astype(F32) * omega_rate
    mass_term = harmonic * harmonic * mass_ref[...]

    def stiffness(ext):
        total = jnp.zeros((RC * 48, BLK), F32)
        for s in range(NNZ):
            code = slots_ref[0, s]
            rows = ext[code // 3, pl.ds(lax.rem(code, 3), RC)].reshape(RC * 48, 128)
            total = total + dot(rows, wide[s].astype(BF16), NT)
        return total

    def finish_halo(ext, copies):
        for copy in copies:
            copy.wait_recv()

        @pl.when(ax == 0)
        def _():
            ext[0] = jnp.zeros(ext.shape[1:], BF16)

        @pl.when(ax == SECTIONS - 1)
        def _():
            ext[2] = jnp.zeros(ext.shape[1:], BF16)

    def smooth(ext):
        total = stiffness(ext)
        for r in range(RC):
            now = cur[r, :, 0:BLK]
            applied = total[r * 48 : (r + 1) * 48] - mass_term * now
            base[r, :, 0:BLK] = now + precond * (rhs_buf[r, :, 0:BLK] - applied)

    finish_halo(ext1, halo1)
    base[...] = jnp.zeros(base.shape, F32)
    smooth(ext1)

    def masks(k):
        code = codes[pl.ds(k, 1), :]
        return [(code == float(r + 1)).astype(F32) for r in range(RC)]

    def take(i):
        for j in range(2):
            k = 2 * i + j
            for c in range(4):
                unpack[j, 24 * c : 24 * c + 24, 0:BLK] = recv_buf[i, 24 * j : 24 * j + 24, c * BLK : (c + 1) * BLK].astype(F32)
            square = unpack[j]
            flat = square[0:BLK].astype(BF16)
            turn = square.T[0:BLK].astype(BF16)
            turned[k] = turn
            mask = masks(k)
            forward = dot(flat, yw[...], NN)
            backward = dot(turn, xw[...], NN)
            kept = jnp.zeros((BLK, SAMPLES), F32)
            for r in range(RC):
                lanes = slice(r * SAMPLES, (r + 1) * SAMPLES)
                kept = kept + forward[:, lanes] * mask[r]
                acc[:, lanes] += backward[:, lanes] * mask[r]
            chosen[k] = kept

    take(0)

    def take_next(i, carry):
        block_copy(i).wait_recv()
        take(i)
        return carry

    lax.fori_loop(1, SECTIONS, take_next, 0)

    def settle(r):
        lanes = slice(r * SAMPLES, (r + 1) * SAMPLES)
        effect = dot(table, acc[:, lanes], NT, HIGHEST) * (2.0 / SAMPLES)
        return base[r, :, 0:BLK] - precond * effect

    for r in range(RC):
        cur[r, :, 0:BLK] = settle(r)
    ext2[1, 1:5] = cur[...].astype(BF16)
    halo2 = halo(ext2, 1)
    for copy in halo2:
        copy.start()
    for r in range(RC):
        lanes = slice(r * SAMPLES, (r + 1) * SAMPLES)
        xw[:, lanes] = spread(ext2[1, 1 + r], mixer).astype(BF16)

    acc[...] = jnp.zeros(acc.shape, F32)

    def again(g, carry):
        k = g * GROUP
        lhs = turned[pl.ds(k, GROUP)].reshape(GROUP * BLK, 128)
        product = dot(lhs, xw[...], NN)
        for j in range(GROUP):
            mask = masks(k + j)
            for r in range(RC):
                lanes = slice(r * SAMPLES, (r + 1) * SAMPLES)
                acc[:, lanes] += product[j * BLK : (j + 1) * BLK, lanes] * mask[r]
        return carry

    lax.fori_loop(0, SLOTS // GROUP, again, 0)
    finish_halo(ext2, halo2)
    smooth(ext2)
    for r in range(RC):
        final = settle(r)
        adj_ref[0, :, r * BLK : (r + 1) * BLK] = final[0:HARM]
        cur[r, :, 0:BLK] = final
    for r in range(RC):
        bw[r] = spread(cur[r].astype(BF16), mixer)[0:BLK]

    def part(k, carry):
        mask = masks(k)
        weight = bw[0] * mask[0]
        for r in range(1, RC):
            weight = weight + bw[r] * mask[r]
        sums[pl.ds(k, 1), :] = jnp.sum(chosen[k] * weight, axis=0, keepdims=True)
        return carry

    lax.fori_loop(0, SLOTS, part, 0)
    parts = jnp.sum(sums[...], axis=1, keepdims=True) * (-sens_scale * 2.0 / SAMPLES)
    own = dot(onehot_hi[...], onehot_lo[...] * parts, NN, HIGHEST)

    def everyone(peers, me, out_of, into, send, recv):
        def copies(j):
            there = lax.rem(me + j, 8)
            going = pltpu.make_async_remote_copy(
                src_ref=out_of(there), dst_ref=into.at[me], send_sem=send.at[j], recv_sem=recv.at[me],
                device_id=peers(there), device_id_type=MESH,
            )
            coming = pltpu.make_async_remote_copy(
                src_ref=out_of(there), dst_ref=into.at[there], send_sem=send.at[j], recv_sem=recv.at[there],
                device_id=peers(there), device_id_type=MESH,
            )
            return going, coming

        pairs = [copies(j) for j in range(1, 8)]
        for going, _ in pairs:
            going.start()
        for _, coming in pairs:
            coming.wait_recv()
        total = into[0]
        for n in range(1, 8):
            total = total + into[n]
        return total, [going for going, _ in pairs]

    part_a[...] = own
    recv_a[ci] = own
    total, sent_a = everyone(lambda j: (ax, j), ci, lambda j: part_a, recv_a, a_send, a_recv)
    for n in range(8):
        part_b[n] = total[n : n + 1]
    recv_b[xy] = part_b[xy]
    total, sent_b = everyone(lambda j: (j * 8 + zz, ci), xy, lambda j: part_b.at[j], recv_b, b_send, b_recv)
    part_c[...] = total
    recv_c[zz] = total
    total, sent_c = everyone(lambda j: (xy * 8 + j, ci), zz, lambda j: part_c, recv_c, c_send, c_recv)
    sens_ref[...] = pltpu.roll(jnp.broadcast_to(total, (8, 128)), lax.rem(128 - 16 * zz, 128), 1)

    for copy in halo1 + halo2 + sent_a + sent_b + sent_c:
        copy.wait_send()

    def drain(i, carry):
        meta_copy(i).wait_send()
        block_copy(i).wait_send()
        return carry

    lax.fori_loop(1, SECTIONS, drain, 0)


def shards(
    lam_start, rhs, state, blocks, slots, mass, precond, contact_blocks, contact_flags,
    contact_owner, contact_row, contact_front,
):
    packed = contact_blocks.reshape(CPD, 24, 384)
    table = jnp.asarray(time_table())
    vmem = pl.BlockSpec(memory_space=pltpu.VMEM)
    smem = pl.BlockSpec(memory_space=pltpu.SMEM)
    dma = pltpu.SemaphoreType.DMA
    scratch = [
        pltpu.VMEM((8, SLOTS), jnp.int32),
        pltpu.SMEM((8, SLOTS), jnp.int32),
        pltpu.VMEM((SECTIONS, 8, 128), BF16),
        pltpu.VMEM((SECTIONS, 8, 128), BF16),
        pltpu.VMEM((SECTIONS, 48, 384), BF16),
        pltpu.VMEM((SECTIONS, 48, 384), BF16),
        pltpu.VMEM((2, 128, 128), F32),
        pltpu.VMEM((SLOTS, BLK, 128), BF16),
        pltpu.VMEM((SLOTS, BLK, SAMPLES), F32),
        pltpu.VMEM((BLK, RC * SAMPLES), F32),
        pltpu.VMEM((SLOTS, 128), F32),
        pltpu.VMEM((SLOTS, 128), F32),
        pltpu.VMEM((SLOTS, 128), F32),
        pltpu.VMEM((8, SLOTS), F32),
        pltpu.VMEM((RC, 48, 128), F32),
        pltpu.VMEM((RC, 48, 128), F32),
        pltpu.VMEM((RC, 48, 128), F32),
        pltpu.VMEM((3, 6, 48, 128), BF16),
        pltpu.VMEM((3, 6, 48, 128), BF16),
        pltpu.VMEM((NNZ, BLK, 128), F32),
        pltpu.VMEM((RC, 48, 128), F32),
        pltpu.VMEM((128, RC * SAMPLES), BF16),
        pltpu.VMEM((128, RC * SAMPLES), BF16),
        pltpu.VMEM((RC, BLK, SAMPLES), F32),
        pltpu.VMEM((SLOTS, 128), F32),
        pltpu.VMEM((8, 128), F32),
        pltpu.VMEM((8, 8, 128), F32),
        pltpu.VMEM((8, 1, 128), F32),
        pltpu.VMEM((8, 1, 128), F32),
        pltpu.VMEM((1, 128), F32),
        pltpu.VMEM((8, 1, 128), F32),
        dma((1,)), dma((SECTIONS,)), dma((SECTIONS,)), dma((SECTIONS,)), dma((SECTIONS,)),
        dma((2, 8)), dma((2, 8)), dma((8,)), dma((8,)), dma((8,)), dma((8,)), dma((8,)), dma((8,)),
    ]
    adjoint, sums = pl.pallas_call(
        kernel,
        out_shape=(
            jax.ShapeDtypeStruct((1, HARM, RC * BLK), F32),
            jax.ShapeDtypeStruct((8, 128), F32),
        ),
        in_specs=[vmem, vmem, vmem, vmem, smem] + [vmem] * 8,
        out_specs=(vmem, vmem),
        scratch_shapes=scratch,
        compiler_params=pltpu.CompilerParams(
            collective_id=0, has_side_effects=True, vmem_limit_bytes=56 * 2**20
        ),
        cost_estimate=pl.CostEstimate(flops=4 * 10**9, bytes_accessed=3 * 10**6, transcendentals=0),
    )(
        lam_start, rhs, state, blocks, slots, mass, precond, packed, contact_flags,
        contact_owner.reshape(1, CPD), contact_row.reshape(1, CPD), contact_front.reshape(1, CPD), table,
    )
    return adjoint, sums[0, :16]


def solution(mesh):
    in_specs = (
        P("ax", None, "circ"),
        P("ax", None, "circ"),
        P("ax", None, "circ"),
        P("ax", None, None),
        P("ax", None),
        P("ax", None),
        P("ax", None),
        P(("ax", "circ"), None),
        P(("ax", "circ"), None),
        P(("ax", "circ")),
        P(("ax", "circ")),
        P(("ax", "circ")),
    )
    out_specs = (P("ax", None, "circ"), P("ax"))
    return jax.shard_map(shards, mesh=mesh, in_specs=in_specs, out_specs=out_specs, check_vma=False)
```

time: 383 us -> 133 us (0.35)
  Pallas kernels: 0 us -> 125 us
  blocking collectives: 110 us -> 0 us
  local copies, waits for them, and re-layouts: 67.7 us -> 5.23 us
  starting transfers between devices: 60.3 us -> 0 us
  waiting for transfers between devices: 56.4 us -> 0 us
  other arithmetic: 36.4 us -> 0 us
  matrix products: 32.6 us -> 0 us
  between operations: 16.8 us -> 0.64 us
    pallas_call x0 -> x1, Pallas kernels: none -> 125 us  [shards(): pl.pallas_call(kernel, out_shape=(jax.ShapeDtypeStruct((1, HARM, RC * BLK...]
    psum x1 -> x0, blocking collectives: 110 us -> none  [shards(): totals = lax.psum(partial_sums, ('ax', 'circ'))]
    all_to_all x4 -> x0, starting transfers between devices: 36.7 us -> none  [the longest x1 19.6 us: shards(): lax.all_to_all(row_buffer, 'ax', split_axis=0, concat_axis=0, tiled=True)]
    dot_general x9 -> x0, matrix products: 32.6 us -> none  [the longest x2 10.2 us: adjoint_effect(): jnp.einsum('khg,gkp->hkp', filters, coupled, precision=lax.Precision.HIGH...]
    all_to_all x4 -> x0, waiting for transfers between devices: 30.1 us -> none  [the longest x1 11.6 us: shards(): lax.all_to_all(front_buffer, 'ax', split_axis=0, concat_axis=0, tiled=True)]
    scatter-add x3 -> x0, other arithmetic: 27.4 us -> none  [the longest x2 25.8 us: add_rows(): shaped.at[wanted // sector_cols, :, wanted % sector_cols, :]]
    ppermute x8 -> x0, waiting for transfers between devices: 26.3 us -> none  [the longest x4 18.3 us: with_halo(): lax.ppermute(lax.slice_in_dim(block, 0, width, axis=dim), axis, backward)]
    ppermute x8 -> x0, starting transfers between devices: 23.6 us -> none  [the longest x4 16.3 us: with_halo(): lax.ppermute(lax.slice_in_dim(block, block.shape[dim] - width, None, axis...]
  transfers between devices with their start and end apart: 12 -> 0, of which waited for: 5 -> 0; matrix products, arithmetic and copies ran while one was open for 14% -> 0% of each run, Pallas kernels for 0% -> 0%
where the time goes in v1:
time: 133 us; the launch traced here: 131 us
  Pallas kernels  125 us (94%)
  local copies, waits for them, and re-layouts  5.23 us (4%)
    pallas_call x1, Pallas kernels, shards(): pl.pallas_call(kernel, out_shape=(jax.ShapeDtypeStruct((1, HARM, RC * BLK...  125 us
    unnamed x2, local copies, waits for them, and re-layouts  4.04 us

profile of v1, /device:TPU:1, one launch (start us, length us, event | category | flops | bytes accessed | tf_op | source)
XLA Modules:
  0.0 131.0 jit_solution(6897840342496248856)
XLA Ops:
  0.6 2.5 %copy.16 = bf16[8,8,24,384]{3,2,1,0:T(8,128)(2,1)} copy(bf16[8,8,24,384]{3,1,2,0:T(8,128)(2,1)} %bitcast.7) | data formatting | bytes 2359296
  3.1 125.1 %shard_map.140 = (f32[1,42,384]{2,1,0:T(8,128)}, f32[8,128]{1,0:T(8,128)}) custom-call(bf16[1,42,384]{2,1,0:T(8,128)(2,1)} %lam_ref.1, bf16[1,42,384]{2,1,0:T(8,128)(2,1)} %rhs_ref.1, bf16[1,42,384]{2,1,0:T(8,128)(2,1)} %state_ref.1, bf16[1,96,768]{2,1,0:T(8,128)(2,1)} %blocks_ref.1, s32[1,8]{1,0:T(1,128)} %slots_ref.1, f32[1,96]{1,0:T(1,128)} %mass_ref.1, ...), custom_call_target="tpu_custom_call" | custom-call | flops 4000000000 | bytes 3000000 | tf_op jit(solution)/shard_map/pallas_call | solution.py:441
  128.2 1.6 %copy.15 = f32[1,42,384]{2,0,1:T(1,128)} copy(f32[1,42,384]{2,1,0:T(8,128)} %get-tuple-element.6) | data formatting | bytes 129024
  129.8 1.2 slice_bitcast_fusion

commit v2 on v1

--- a/solution.py
+++ b/solution.py
@@ -18,7 +18,10 @@
 SECTORS = 8
 SLOTS = 2 * SECTIONS
 STEP = 29
-GROUP = 4
+GROUP = 8
+WINDOW = 16
+LEN = 72
+MSG = 2 * LEN + 8
 
 omega_rate = 0.05
 sens_scale = 0.015625
@@ -54,10 +57,10 @@
     lam_ref, rhs_ref, state_ref, blocks_ref, slots_ref, mass_ref, precond_ref, contacts_ref,
     flags_ref, owner_ref, row_ref, front_ref, table_ref,
     adj_ref, sens_ref,
-    idx_v, idx_s, meta_out, meta_in, send_buf, recv_buf, unpack, turned, chosen, acc, codes, fronts,
+    idx_v, idx_s, meta_out, send_buf, recv_buf, unpack, turned, chosen, acc, codes, fronts,
     onehot_lo, onehot_hi, rhs_buf, cur, base, ext1, ext2, wide, state_pad, xw, yw, bw, sums,
     part_a, recv_a, part_b, recv_b, part_c, recv_c,
-    local_sem, meta_send, meta_recv, block_send, block_recv, halo_send, halo_recv,
+    local_sem, block_send, block_recv, halo_send, halo_recv,
     a_send, a_recv, b_send, b_recv, c_send, c_recv,
 ):
     ax = lax.axis_index("ax")
@@ -154,37 +157,27 @@
     for copy in halo1:
         copy.start()
 
-    def meta_copy(i):
-        return pltpu.make_async_remote_copy(
-            src_ref=meta_out.at[ax_peer(i)], dst_ref=meta_in.at[i], send_sem=meta_send.at[i],
-            recv_sem=meta_recv.at[i], device_id=(ax_peer(i), ci), device_id_type=MESH,
-        )
-
     def block_copy(i):
         return pltpu.make_async_remote_copy(
             src_ref=send_buf.at[i], dst_ref=recv_buf.at[i], send_sem=block_send.at[i],
             recv_sem=block_recv.at[i], device_id=(ax_peer(i), ci), device_id_type=MESH,
         )
 
-    def start_meta(i, carry):
-        meta_copy(i).start()
-        return carry
-
     to_scalar.wait()
 
+    def fill(buf, i):
+        slot = 2 * ax_peer(i)
+        buf[i, 0:LEN, :] = contacts_ref[idx_s[0, slot]]
+        buf[i, LEN : 2 * LEN, :] = contacts_ref[idx_s[0, slot + 1]]
+        buf[i, 2 * LEN : MSG, :] = meta_out[ax_peer(i)]
+
     def start_block(i, carry):
-        slot = 2 * ax_peer(i)
-        send_buf[i, 0:24, :] = contacts_ref[idx_s[0, slot]]
-        send_buf[i, 24:48, :] = contacts_ref[idx_s[0, slot + 1]]
+        fill(send_buf, i)
         block_copy(i).start()
         return carry
 
-    lax.fori_loop(1, 9, start_block, 0)
-    lax.fori_loop(1, SECTIONS, start_meta, 0)
-    lax.fori_loop(9, SECTIONS, start_block, 0)
-    recv_buf[0, 0:24, :] = contacts_ref[idx_s[0, 2 * ax]]
-    recv_buf[0, 24:48, :] = contacts_ref[idx_s[0, 2 * ax + 1]]
-    meta_in[0] = meta_out[ax]
+    lax.fori_loop(1, WINDOW + 1, start_block, 0)
+    fill(recv_buf, 0)
 
     spot = iota((128, 128), 0)
     mixed = (iota((128, 128), 1) == 4 * lax.rem(spot, 24) + spot // 24) & (spot < BLK)
@@ -198,38 +191,25 @@
         turn = dot(order, rows, NT).astype(BF16)
         return dot(turn, table_hi, NN) + dot(turn, table_lo, NN)
 
+    def split(ref, lanes, value):
+        first = value.astype(BF16)
+        ref[0:128, lanes] = first
+        ref[128:256, lanes] = (value - first.astype(F32)).astype(BF16)
+
+    def twice(x):
+        return jnp.concatenate([x, x], axis=1)
+
     pad_rows(state_pad, state_ref)
     for r in range(RC):
         lanes = slice(r * SAMPLES, (r + 1) * SAMPLES)
-        xw[:, lanes] = spread(ext1[1, 1 + r], mixer).astype(BF16)
-        yw[:, lanes] = spread(state_pad[r].astype(BF16), plain).astype(BF16)
+        split(xw, lanes, spread(ext1[1, 1 + r], mixer))
+        split(yw, lanes, spread(state_pad[r].astype(BF16), plain))
     pad_rows(rhs_buf, rhs_ref)
     wide[...] = jnp.zeros(wide.shape, F32)
     for s in range(NNZ):
         wide[s, :, 0:BLK] = blocks_ref[0, :, s * BLK : (s + 1) * BLK].astype(F32)
     acc[...] = jnp.zeros(acc.shape, F32)
     unpack[...] = jnp.zeros(unpack.shape, F32)
-
-    def wait_meta(i, carry):
-        meta_copy(i).wait_recv()
-        return carry
-
-    lax.fori_loop(1, SECTIONS, wait_meta, 0)
-
-    def spread_meta(i, carry):
-        rows = meta_in[i].astype(F32)
-        codes[pl.ds(2 * i, 2), :] = rows[0:2]
-        fronts[pl.ds(2 * i, 2), :] = rows[2:4]
-        return carry
-
-    lax.fori_loop(0, SECTIONS, spread_meta, 0)
-    eye128 = (spot == iota((128, 128), 1)).astype(F32)
-    high, low = fronts[:, 0:1], fronts[:, 64:65]
-    major = jnp.floor(high * 0.25)
-    minor = (high - 4.0 * major) * 32.0 + low
-    onehot_lo[...] = (minor == iota((128, 128), 1).astype(F32)).astype(F32)
-    major_row = jnp.sum(eye128 * major, axis=0, keepdims=True)
-    onehot_hi[...] = (major_row == iota((8, 128), 0).astype(F32)).astype(F32)
 
     precond = precond_ref[...]
     harmonic = (iota((48, BLK), 0) // 2 + 1).astype(F32) * omega_rate
@@ -271,17 +251,22 @@
         return [(code == float(r + 1)).astype(F32) for r in range(RC)]
 
     def take(i):
+        meta = recv_buf[i, 2 * LEN : MSG, :].astype(F32)
+        codes[pl.ds(2 * i, 2), :] = meta[0:2]
+        fronts[pl.ds(2 * i, 2), :] = meta[2:4]
         for j in range(2):
             k = 2 * i + j
+            pieces = [recv_buf[i, LEN * j + 24 * c : LEN * j + 24 * c + 24, :] for c in range(3)]
+            square = jnp.concatenate(pieces, axis=1).astype(F32)
             for c in range(4):
-                unpack[j, 24 * c : 24 * c + 24, 0:BLK] = recv_buf[i, 24 * j : 24 * j + 24, c * BLK : (c + 1) * BLK].astype(F32)
+                unpack[j, 24 * c : 24 * c + 24, 0:BLK] = square[:, c * BLK : (c + 1) * BLK]
             square = unpack[j]
             flat = square[0:BLK].astype(BF16)
             turn = square.T[0:BLK].astype(BF16)
             turned[k] = turn
-            mask = masks(k)
-            forward = dot(flat, yw[...], NN)
-            backward = dot(turn, xw[...], NN)
+            mask = [(meta[j : j + 1] == float(r + 1)).astype(F32) for r in range(RC)]
+            forward = dot(twice(flat), yw[...], NN)
+            backward = dot(twice(turn), xw[...], NN)
             kept = jnp.zeros((BLK, SAMPLES), F32)
             for r in range(RC):
                 lanes = slice(r * SAMPLES, (r + 1) * SAMPLES)
@@ -291,12 +276,20 @@
 
     take(0)
 
+    def pass_on(i, carry):
+        block_copy(i).wait_send()
+        start_block(i + WINDOW, carry)
+        block_copy(i).wait_recv()
+        take(i)
+        return carry
+
     def take_next(i, carry):
         block_copy(i).wait_recv()
         take(i)
         return carry
 
-    lax.fori_loop(1, SECTIONS, take_next, 0)
+    lax.fori_loop(1, SECTIONS - WINDOW, pass_on, 0)
+    lax.fori_loop(SECTIONS - WINDOW, SECTIONS, take_next, 0)
 
     def settle(r):
         lanes = slice(r * SAMPLES, (r + 1) * SAMPLES)
@@ -311,22 +304,31 @@
         copy.start()
     for r in range(RC):
         lanes = slice(r * SAMPLES, (r + 1) * SAMPLES)
-        xw[:, lanes] = spread(ext2[1, 1 + r], mixer).astype(BF16)
+        split(xw, lanes, spread(ext2[1, 1 + r], mixer))
 
     acc[...] = jnp.zeros(acc.shape, F32)
 
     def again(g, carry):
         k = g * GROUP
         lhs = turned[pl.ds(k, GROUP)].reshape(GROUP * BLK, 128)
-        product = dot(lhs, xw[...], NN)
-        for j in range(GROUP):
-            mask = masks(k + j)
-            for r in range(RC):
-                lanes = slice(r * SAMPLES, (r + 1) * SAMPLES)
-                acc[:, lanes] += product[j * BLK : (j + 1) * BLK, lanes] * mask[r]
+        product = dot(twice(lhs), xw[...], NN)
+        mask = [masks(k + j) for j in range(GROUP)]
+        for r in range(RC):
+            lanes = slice(r * SAMPLES, (r + 1) * SAMPLES)
+            total = acc[:, lanes]
+            for j in range(GROUP):
+                total = total + product[j * BLK : (j + 1) * BLK, lanes] * mask[j][r]
+            acc[:, lanes] = total
         return carry
 
     lax.fori_loop(0, SLOTS // GROUP, again, 0)
+    eye128 = (spot == iota((128, 128), 1)).astype(F32)
+    high, low = fronts[:, 0:1], fronts[:, 64:65]
+    major = jnp.floor(high * 0.25)
+    minor = (high - 4.0 * major) * 32.0 + low
+    onehot_lo[...] = (minor == iota((128, 128), 1).astype(F32)).astype(F32)
+    major_row = jnp.sum(eye128 * major, axis=0, keepdims=True)
+    onehot_hi[...] = (major_row == iota((8, 128), 0).astype(F32)).astype(F32)
     finish_halo(ext2, halo2)
     smooth(ext2)
     for r in range(RC):
@@ -336,15 +338,15 @@
     for r in range(RC):
         bw[r] = spread(cur[r].astype(BF16), mixer)[0:BLK]
 
-    def part(k, carry):
-        mask = masks(k)
-        weight = bw[0] * mask[0]
-        for r in range(1, RC):
-            weight = weight + bw[r] * mask[r]
-        sums[pl.ds(k, 1), :] = jnp.sum(chosen[k] * weight, axis=0, keepdims=True)
-        return carry
-
-    lax.fori_loop(0, SLOTS, part, 0)
+    def part(g, carry):
+        for j in range(4):
+            k = 4 * g + j
+            code = jnp.broadcast_to(codes[pl.ds(k, 1), :], (BLK, SAMPLES))
+            weight = jnp.where(code == 1.0, bw[0], jnp.where(code == 2.0, bw[1], jnp.where(code == 3.0, bw[2], bw[3])))
+            sums[pl.ds(k, 1), :] = jnp.sum(chosen[k] * weight, axis=0, keepdims=True)
+        return carry
+
+    lax.fori_loop(0, SLOTS // 4, part, 0)
     parts = jnp.sum(sums[...], axis=1, keepdims=True) * (-sens_scale * 2.0 / SAMPLES)
     own = dot(onehot_hi[...], onehot_lo[...] * parts, NN, HIGHEST)
 
@@ -387,18 +389,17 @@
         copy.wait_send()
 
     def drain(i, carry):
-        meta_copy(i).wait_send()
         block_copy(i).wait_send()
         return carry
 
-    lax.fori_loop(1, SECTIONS, drain, 0)
+    lax.fori_loop(SECTIONS - WINDOW, SECTIONS, drain, 0)
 
 
 def shards(
     lam_start, rhs, state, blocks, slots, mass, precond, contact_blocks, contact_flags,
     contact_owner, contact_row, contact_front,
 ):
-    packed = contact_blocks.reshape(CPD, 24, 384)
+    packed = contact_blocks.reshape(CPD, 24, 3, 128).transpose(0, 2, 1, 3).reshape(CPD, LEN, 128)
     table = jnp.asarray(time_table())
     vmem = pl.BlockSpec(memory_space=pltpu.VMEM)
     smem = pl.BlockSpec(memory_space=pltpu.SMEM)
@@ -407,9 +408,8 @@
         pltpu.VMEM((8, SLOTS), jnp.int32),
         pltpu.SMEM((8, SLOTS), jnp.int32),
         pltpu.VMEM((SECTIONS, 8, 128), BF16),
-        pltpu.VMEM((SECTIONS, 8, 128), BF16),
-        pltpu.VMEM((SECTIONS, 48, 384), BF16),
-        pltpu.VMEM((SECTIONS, 48, 384), BF16),
+        pltpu.VMEM((SECTIONS, MSG, 128), BF16),
+        pltpu.VMEM((SECTIONS, MSG, 128), BF16),
         pltpu.VMEM((2, 128, 128), F32),
         pltpu.VMEM((SLOTS, BLK, 128), BF16),
         pltpu.VMEM((SLOTS, BLK, SAMPLES), F32),
@@ -425,8 +425,8 @@
         pltpu.VMEM((3, 6, 48, 128), BF16),
         pltpu.VMEM((NNZ, BLK, 128), F32),
         pltpu.VMEM((RC, 48, 128), F32),
-        pltpu.VMEM((128, RC * SAMPLES), BF16),
-        pltpu.VMEM((128, RC * SAMPLES), BF16),
+        pltpu.VMEM((256, RC * SAMPLES), BF16),
+        pltpu.VMEM((256, RC * SAMPLES), BF16),
         pltpu.VMEM((RC, BLK, SAMPLES), F32),
         pltpu.VMEM((SLOTS, 128), F32),
         pltpu.VMEM((8, 128), F32),
@@ -435,7 +435,7 @@
         pltpu.VMEM((8, 1, 128), F32),
         pltpu.VMEM((1, 128), F32),
         pltpu.VMEM((8, 1, 128), F32),
-        dma((1,)), dma((SECTIONS,)), dma((SECTIONS,)), dma((SECTIONS,)), dma((SECTIONS,)),
+        dma((1,)), dma((SECTIONS,)), dma((SECTIONS,)),
         dma((2, 8)), dma((2, 8)), dma((8,)), dma((8,)), dma((8,)), dma((8,)), dma((8,)), dma((8,)),
     ]
     adjoint, sums = pl.pallas_call(

time: 133 us -> 124 us (0.932); the launches traced: 131 us -> 124 us
  Pallas kernels: 125 us -> 116 us
  local copies, waits for them, and re-layouts: 5.23 us -> 7.19 us
    pallas_call x1, Pallas kernels: 125 us -> 116 us  [shards(): pl.pallas_call(kernel, out_shape=(jax.ShapeDtypeStruct((1, HARM, RC * BLK...]
    reshape x0 -> x1, local copies, waits for them, and re-layouts: none -> 3.24 us  [shards(): contact_blocks.reshape(CPD, 24, 3, 128).transpose(0, 2, 1, 3)]
    unnamed x2 -> x1, local copies, waits for them, and re-layouts: 4.04 us -> 1.58 us
where the time goes in v2:
time: 124 us
  Pallas kernels  116 us (94%)
  local copies, waits for them, and re-layouts  7.19 us (6%)
    pallas_call x1, Pallas kernels, shards(): pl.pallas_call(kernel, out_shape=(jax.ShapeDtypeStruct((1, HARM, RC * BLK...  116 us
    reshape x1, local copies, waits for them, and re-layouts, shards(): contact_blocks.reshape(CPD, 24, 3, 128).transpose(0, 2, 1, 3)  3.24 us

profile of v2, /device:TPU:1, one launch (start us, length us, event | category | flops | bytes accessed | tf_op | source)
XLA Modules:
  0.0 123.8 jit_solution(16289731885871616718)
XLA Ops:
  0.6 3.2 %reshape.19 = bf16[64,24,3,128]{3,2,1,0:T(4,128)(2,1)S(1)} reshape(bf16[64,9216]{1,0:T(8,128)(2,1)} %param.20) | data formatting | bytes 2359296 | tf_op jit(solution)/shard_map/reshape | solution.py:402
  3.9 1.2 copy.17
  5.1 116.0 %shard_map.140 = (f32[1,42,384]{2,1,0:T(8,128)}, f32[8,128]{1,0:T(8,128)}) custom-call(bf16[1,42,384]{2,1,0:T(8,128)(2,1)} %lam_ref.1, bf16[1,42,384]{2,1,0:T(8,128)(2,1)} %rhs_ref.1, bf16[1,42,384]{2,1,0:T(8,128)(2,1)} %state_ref.1, bf16[1,96,768]{2,1,0:T(8,128)(2,1)} %blocks_ref.1, s32[1,8]{1,0:T(1,128)} %slots_ref.1, f32[1,96]{1,0:T(1,128)} %mass_ref.1, ...), custom_call_target="tpu_custom_call" | custom-call | flops 4000000000 | bytes 3000000 | tf_op jit(solution)/shard_map/pallas_call | solution.py:441
  121.1 1.6 %copy.18 = f32[1,42,384]{2,0,1:T(1,128)} copy(f32[1,42,384]{2,1,0:T(8,128)} %get-tuple-element.8) | data formatting | bytes 129024
  122.7 1.2 slice_bitcast_fusion

commit v3 on v2

--- a/solution.py
+++ b/solution.py
@@ -20,6 +20,7 @@
 STEP = 29
 GROUP = 8
 WINDOW = 16
+EARLY = 20
 LEN = 72
 MSG = 2 * LEN + 8
 
@@ -58,7 +59,7 @@
     flags_ref, owner_ref, row_ref, front_ref, table_ref,
     adj_ref, sens_ref,
     idx_v, idx_s, meta_out, send_buf, recv_buf, unpack, turned, chosen, acc, codes, fronts,
-    onehot_lo, onehot_hi, rhs_buf, cur, base, ext1, ext2, wide, state_pad, xw, yw, bw, sums,
+    onehot_lo, onehot_hi, rhs_buf, cur, base, ext1, ext2, wide, state_pad, xw, yw, tables, bw, sums,
     part_a, recv_a, part_b, recv_b, part_c, recv_c,
     local_sem, block_send, block_recv, halo_send, halo_recv,
     a_send, a_recv, b_send, b_recv, c_send, c_recv,
@@ -187,27 +188,26 @@
     table_hi = table.astype(BF16)
     table_lo = (table - table_hi.astype(F32)).astype(BF16)
 
+    tables[...] = jnp.zeros(tables.shape, BF16)
+    for r in range(RC):
+        tables[0, 48 * r : 48 * r + 48, r * SAMPLES : (r + 1) * SAMPLES] = table_hi
+        tables[1, 48 * r : 48 * r + 48, r * SAMPLES : (r + 1) * SAMPLES] = table_lo
+
     def spread(rows, order):
-        turn = dot(order, rows, NT).astype(BF16)
-        return dot(turn, table_hi, NN) + dot(turn, table_lo, NN)
-
-    def split(ref, lanes, value):
+        turn = dot(order, rows.reshape(RC * 48, 128), NT).astype(BF16)
+        return dot(turn, tables[0], NN) + dot(turn, tables[1], NN)
+
+    def split(ref, value):
         first = value.astype(BF16)
-        ref[0:128, lanes] = first
-        ref[128:256, lanes] = (value - first.astype(F32)).astype(BF16)
+        ref[0:128, :] = first
+        ref[128:256, :] = (value - first.astype(F32)).astype(BF16)
 
     def twice(x):
         return jnp.concatenate([x, x], axis=1)
 
     pad_rows(state_pad, state_ref)
-    for r in range(RC):
-        lanes = slice(r * SAMPLES, (r + 1) * SAMPLES)
-        split(xw, lanes, spread(ext1[1, 1 + r], mixer))
-        split(yw, lanes, spread(state_pad[r].astype(BF16), plain))
-    pad_rows(rhs_buf, rhs_ref)
-    wide[...] = jnp.zeros(wide.shape, F32)
-    for s in range(NNZ):
-        wide[s, :, 0:BLK] = blocks_ref[0, :, s * BLK : (s + 1) * BLK].astype(F32)
+    split(xw, spread(ext1[1, 1:5], mixer))
+    split(yw, spread(state_pad[...].astype(BF16), plain))
     acc[...] = jnp.zeros(acc.shape, F32)
     unpack[...] = jnp.zeros(unpack.shape, F32)
 
@@ -241,10 +241,6 @@
             now = cur[r, :, 0:BLK]
             applied = total[r * 48 : (r + 1) * 48] - mass_term * now
             base[r, :, 0:BLK] = now + precond * (rhs_buf[r, :, 0:BLK] - applied)
-
-    finish_halo(ext1, halo1)
-    base[...] = jnp.zeros(base.shape, F32)
-    smooth(ext1)
 
     def masks(k):
         code = codes[pl.ds(k, 1), :]
@@ -288,24 +284,31 @@
         take(i)
         return carry
 
-    lax.fori_loop(1, SECTIONS - WINDOW, pass_on, 0)
+    lax.fori_loop(1, EARLY, pass_on, 0)
+    pad_rows(rhs_buf, rhs_ref)
+    wide[...] = jnp.zeros(wide.shape, F32)
+    for s in range(NNZ):
+        wide[s, :, 0:BLK] = blocks_ref[0, :, s * BLK : (s + 1) * BLK].astype(F32)
+    finish_halo(ext1, halo1)
+    smooth(ext1)
+    lax.fori_loop(EARLY, SECTIONS - WINDOW, pass_on, 0)
     lax.fori_loop(SECTIONS - WINDOW, SECTIONS, take_next, 0)
 
-    def settle(r):
-        lanes = slice(r * SAMPLES, (r + 1) * SAMPLES)
-        effect = dot(table, acc[:, lanes], NT, HIGHEST) * (2.0 / SAMPLES)
-        return base[r, :, 0:BLK] - precond * effect
-
-    for r in range(RC):
-        cur[r, :, 0:BLK] = settle(r)
+    def settle():
+        rows = jnp.concatenate([acc[:, r * SAMPLES : (r + 1) * SAMPLES] for r in range(RC)], axis=0)
+        first = rows.astype(BF16)
+        second = (rows - first.astype(F32)).astype(BF16)
+        left = jnp.concatenate([table_hi, table_lo, table_hi], axis=1)
+        effect = dot(left, jnp.concatenate([first, first, second], axis=1), NT) * (2.0 / SAMPLES)
+        return [base[r, :, 0:BLK] - precond * effect[:, r * BLK : (r + 1) * BLK] for r in range(RC)]
+
+    for r, value in enumerate(settle()):
+        cur[r, :, 0:BLK] = value
     ext2[1, 1:5] = cur[...].astype(BF16)
     halo2 = halo(ext2, 1)
     for copy in halo2:
         copy.start()
-    for r in range(RC):
-        lanes = slice(r * SAMPLES, (r + 1) * SAMPLES)
-        split(xw, lanes, spread(ext2[1, 1 + r], mixer))
-
+    split(xw, spread(ext2[1, 1:5], mixer))
     acc[...] = jnp.zeros(acc.shape, F32)
 
     def again(g, carry):
@@ -331,18 +334,17 @@
     onehot_hi[...] = (major_row == iota((8, 128), 0).astype(F32)).astype(F32)
     finish_halo(ext2, halo2)
     smooth(ext2)
-    for r in range(RC):
-        final = settle(r)
-        adj_ref[0, :, r * BLK : (r + 1) * BLK] = final[0:HARM]
-        cur[r, :, 0:BLK] = final
-    for r in range(RC):
-        bw[r] = spread(cur[r].astype(BF16), mixer)[0:BLK]
+    for r, value in enumerate(settle()):
+        adj_ref[0, :, r * BLK : (r + 1) * BLK] = value[0:HARM]
+        cur[r, :, 0:BLK] = value
+    bw[...] = spread(cur[...].astype(BF16), mixer)[0:BLK]
 
     def part(g, carry):
         for j in range(4):
             k = 4 * g + j
             code = jnp.broadcast_to(codes[pl.ds(k, 1), :], (BLK, SAMPLES))
-            weight = jnp.where(code == 1.0, bw[0], jnp.where(code == 2.0, bw[1], jnp.where(code == 3.0, bw[2], bw[3])))
+            rows = [bw[:, r * SAMPLES : (r + 1) * SAMPLES] for r in range(RC)]
+            weight = jnp.where(code == 1.0, rows[0], jnp.where(code == 2.0, rows[1], jnp.where(code == 3.0, rows[2], rows[3])))
             sums[pl.ds(k, 1), :] = jnp.sum(chosen[k] * weight, axis=0, keepdims=True)
         return carry
 
@@ -393,6 +395,11 @@
         return carry
 
     lax.fori_loop(SECTIONS - WINDOW, SECTIONS, drain, 0)
+
+
+def finish(adj_ref, sums_ref, adj_out, sens_out):
+    adj_out[:, 0, :] = adj_ref[0]
+    sens_out[...] = sums_ref[0, 0:16]
 
 
 def shards(
@@ -427,7 +434,8 @@
         pltpu.VMEM((RC, 48, 128), F32),
         pltpu.VMEM((256, RC * SAMPLES), BF16),
         pltpu.VMEM((256, RC * SAMPLES), BF16),
-        pltpu.VMEM((RC, BLK, SAMPLES), F32),
+        pltpu.VMEM((2, RC * 48, RC * SAMPLES), BF16),
+        pltpu.VMEM((BLK, RC * SAMPLES), F32),
         pltpu.VMEM((SLOTS, 128), F32),
         pltpu.VMEM((8, 128), F32),
         pltpu.VMEM((8, 8, 128), F32),
@@ -455,7 +463,16 @@
         lam_start, rhs, state, blocks, slots, mass, precond, packed, contact_flags,
         contact_owner.reshape(1, CPD), contact_row.reshape(1, CPD), contact_front.reshape(1, CPD), table,
     )
-    return adjoint, sums[0, :16]
+    adjoint, sums = pl.pallas_call(
+        finish,
+        out_shape=(
+            jax.ShapeDtypeStruct((HARM, 1, RC * BLK), F32),
+            jax.ShapeDtypeStruct((16,), F32),
+        ),
+        in_specs=[vmem, vmem],
+        out_specs=(vmem, vmem),
+    )(adjoint, sums)
+    return adjoint.transpose(1, 0, 2), sums
 
 
 def solution(mesh):

time: 124 us -> 119 us (0.960)
  Pallas kernels: 116 us -> 113 us
  local copies, waits for them, and re-layouts: 7.19 us -> 4.43 us
    pallas_call x1, Pallas kernels: 116 us -> 112 us  [shards(): pl.pallas_call(kernel, out_shape=(jax.ShapeDtypeStruct((1, HARM, RC * BLK...]
    unnamed x1 -> x0, local copies, waits for them, and re-layouts: 1.58 us -> none
    pallas_call x0 -> x1, Pallas kernels: none -> 1.53 us  [shards(): pl.pallas_call(finish, out_shape=(jax.ShapeDtypeStruct((HARM, 1, RC * BLK...]
where the time goes in v3:
time: 119 us
  Pallas kernels  113 us (95%)
  local copies, waits for them, and re-layouts  4.43 us (4%)
    pallas_call x1, Pallas kernels, shards(): pl.pallas_call(kernel, out_shape=(jax.ShapeDtypeStruct((1, HARM, RC * BLK...  112 us
    reshape x1, local copies, waits for them, and re-layouts, shards(): contact_blocks.reshape(CPD, 24, 3, 128).transpose(0, 2, 1, 3)  3.24 us

profile of v3, /device:TPU:1, one launch (start us, length us, event | category | flops | bytes accessed | tf_op | source)
XLA Modules:
  0.0 118.5 jit_solution(2501039137715428284)
XLA Ops:
  0.6 3.2 %reshape.19 = bf16[64,24,3,128]{3,2,1,0:T(4,128)(2,1)S(1)} reshape(bf16[64,9216]{1,0:T(8,128)(2,1)} %param.20) | data formatting | bytes 2359296 | tf_op jit(solution)/shard_map/reshape | solution.py:409
  3.9 1.2 %copy.16 = bf16[64,3,24,128]{3,2,1,0:T(8,128)(2,1)} copy(bf16[64,3,24,128]{3,1,2,0:T(4,128)(2,1)S(1)} %bitcast.6) | data formatting | bytes 2359296 | tf_op jit(solution)/shard_map/transpose | solution.py:409
  5.1 111.9 %shard_map.140 = (f32[1,42,384]{2,1,0:T(8,128)}, f32[8,128]{1,0:T(8,128)}) custom-call(bf16[1,42,384]{2,1,0:T(8,128)(2,1)} %lam_ref.1, bf16[1,42,384]{2,1,0:T(8,128)(2,1)} %rhs_ref.1, bf16[1,42,384]{2,1,0:T(8,128)(2,1)} %state_ref.1, bf16[1,96,768]{2,1,0:T(8,128)(2,1)} %blocks_ref.1, s32[1,8]{1,0:T(1,128)} %slots_ref.1, f32[1,96]{1,0:T(1,128)} %mass_ref.1, ...), custom_call_target="tpu_custom_call" | custom-call | flops 4000000000 | bytes 3000000 | tf_op jit(solution)/shard_map/pallas_call | solution.py:449
  117.0 1.5 %shard_map.141 = (f32[42,1,384]{2,1,0:T(1,128)}, f32[16]{0:T(128)}) custom-call(f32[1,42,384]{2,1,0:T(8,128)} %get-tuple-element.6.adj_ref, f32[8,128]{1,0:T(8,128)} %get-tuple-element.7.sums_ref), custom_call_target="tpu_custom_call" | custom-call | tf_op jit(solution)/shard_map/pallas_call | solution.py:466

commit v4 on v3

--- a/solution.py
+++ b/solution.py
@@ -340,15 +340,15 @@
     bw[...] = spread(cur[...].astype(BF16), mixer)[0:BLK]
 
     def part(g, carry):
-        for j in range(4):
-            k = 4 * g + j
+        for j in range(8):
+            k = 8 * g + j
             code = jnp.broadcast_to(codes[pl.ds(k, 1), :], (BLK, SAMPLES))
             rows = [bw[:, r * SAMPLES : (r + 1) * SAMPLES] for r in range(RC)]
             weight = jnp.where(code == 1.0, rows[0], jnp.where(code == 2.0, rows[1], jnp.where(code == 3.0, rows[2], rows[3])))
             sums[pl.ds(k, 1), :] = jnp.sum(chosen[k] * weight, axis=0, keepdims=True)
         return carry
 
-    lax.fori_loop(0, SLOTS // 4, part, 0)
+    lax.fori_loop(0, SLOTS // 8, part, 0)
     parts = jnp.sum(sums[...], axis=1, keepdims=True) * (-sens_scale * 2.0 / SAMPLES)
     own = dot(onehot_hi[...], onehot_lo[...] * parts, NN, HIGHEST)
 

time: 119 us -> 119 us (level)
  no operation moved by 1% of the time
where the time goes in v4:
time: 119 us; the launch traced here: 118 us
  Pallas kernels  113 us (95%)
  local copies, waits for them, and re-layouts  4.43 us (4%)
    pallas_call x1, Pallas kernels, shards(): pl.pallas_call(kernel, out_shape=(jax.ShapeDtypeStruct((1, HARM, RC * BLK...  112 us
    reshape x1, local copies, waits for them, and re-layouts, shards(): contact_blocks.reshape(CPD, 24, 3, 128).transpose(0, 2, 1, 3)  3.24 us

profile of v4, /device:TPU:1, one launch (start us, length us, event | category | flops | bytes accessed | tf_op | source)
XLA Modules:
  0.0 118.5 jit_solution(7773960665050808203)
XLA Ops:
  0.6 3.2 %reshape.19 = bf16[64,24,3,128]{3,2,1,0:T(4,128)(2,1)S(1)} reshape(bf16[64,9216]{1,0:T(8,128)(2,1)} %param.20) | data formatting | bytes 2359296 | tf_op jit(solution)/shard_map/reshape | solution.py:409
  3.9 1.2 %copy.16 = bf16[64,3,24,128]{3,2,1,0:T(8,128)(2,1)} copy(bf16[64,3,24,128]{3,1,2,0:T(4,128)(2,1)S(1)} %bitcast.6) | data formatting | bytes 2359296 | tf_op jit(solution)/shard_map/transpose | solution.py:409
  5.1 111.8 %shard_map.140 = (f32[1,42,384]{2,1,0:T(8,128)}, f32[8,128]{1,0:T(8,128)}) custom-call(bf16[1,42,384]{2,1,0:T(8,128)(2,1)} %lam_ref.1, bf16[1,42,384]{2,1,0:T(8,128)(2,1)} %rhs_ref.1, bf16[1,42,384]{2,1,0:T(8,128)(2,1)} %state_ref.1, bf16[1,96,768]{2,1,0:T(8,128)(2,1)} %blocks_ref.1, s32[1,8]{1,0:T(1,128)} %slots_ref.1, f32[1,96]{1,0:T(1,128)} %mass_ref.1, ...), custom_call_target="tpu_custom_call" | custom-call | flops 4000000000 | bytes 3000000 | tf_op jit(solution)/shard_map/pallas_call | solution.py:449
  116.9 1.5 %shard_map.141 = (f32[42,1,384]{2,1,0:T(1,128)}, f32[16]{0:T(128)}) custom-call(f32[1,42,384]{2,1,0:T(8,128)} %get-tuple-element.6.adj_ref, f32[8,128]{1,0:T(8,128)} %get-tuple-element.7.sums_ref), custom_call_target="tpu_custom_call" | custom-call | tf_op jit(solution)/shard_map/pallas_call | solution.py:466
